TPU v7x, 32 devices: a whole 2x2x4 slice. The times are simulated.
32 devices in a mesh: head: 2 (over x), blk: 16 (over z, y, core).
Axes of the slice: x: 2, y: 2, z: 4, core: 2. Of those that a mesh axis runs over, the one named last changes fastest.
Arguments:
- queries: bfloat16 [2, 6144, 5120], P('head', 'blk'), may hold values from -8 to 8
- keys: bfloat16 [2, 6144, 5120], P('head', 'blk'), may hold values from -8 to 8
- values: bfloat16 [2, 6144, 5120], P('head', 'blk'), may hold values from -6 to 6
- q_gain: float32 [5120], replicated, may hold values from 0.1 to 1.9
- k_gain: float32 [5120], replicated, may hold values from 0.1 to 1.9
- slopes: float32 [40], P('head'), may hold values from 0.25 to 4
- out_weight: bfloat16 [5120, 5120], P('head', 'blk'), may hold values from -1 to 1
- kv_tiles: int32 [32, 4], replicated, may hold values from 0 to 31, as said below
- tile_frame: int32 [32], replicated, may hold values from 0 to 3, never falling along the last dimension, each value on 1 to 16 neighbouring positions
Outputs:
- mixed: bfloat16 [2, 6144, 5120], P('head', 'blk')
Inputs may be any that keep to these rules, and one draw needn't show every extreme that they name: kv_tiles[t, 0] = t; the other entries of row t are distinct tiles other than t, each within 3 tiles of t. `tile_frame`: never falls from one tile to the next.
All inputs are finite; a program needn't handle non-finite values.
Results may differ from a plain program's by a relative error of at most 0.013.
Values may be sent and summed in bfloat16 or wider, within the bound.
A program may use at most 256 MiB of HBM per device.

v0:
```python
import jax
import jax.numpy as jnp
from jax import lax
from jax.sharding import PartitionSpec as P

HEADS = 40
HDIM = 128
TILE = 384


def passed_along(value, axis, steps):
    count = lax.axis_size(axis)
    initial, last = (max(0, -steps), min(count, count - steps))
    return lax.ppermute(value, axis, [(source, source + steps) for source in range(initial, last)])


def rms_norm(rows, gain):
    floats = rows.astype(jnp.float32)
    factor = lax.rsqrt(jnp.mean(floats * floats, axis=-1, keepdims=True) + 1e-06)
    return (floats * factor * gain).astype(jnp.bfloat16)


def shards(queries, keys, values, q_gain, k_gain, slopes, out_weight, kv_tiles, tile_frame):
    position = lax.axis_index("blk")
    query_normed = rms_norm(queries[0], q_gain)
    key_normed = rms_norm(keys[0], k_gain)
    tok_rows = query_normed.shape[0]
    by_head = (
        query_normed.reshape(tok_rows, HEADS, HDIM),
        key_normed.reshape(tok_rows, HEADS, HDIM),
        values[0].reshape(tok_rows, HEADS, HDIM),
    )
    query_heads, key_heads, value_heads = (
        lax.all_to_all(by_head[0], "head", split_axis=1, concat_axis=0, tiled=True),
        lax.all_to_all(by_head[1], "head", split_axis=1, concat_axis=0, tiled=True),
        lax.all_to_all(by_head[2], "head", split_axis=1, concat_axis=0, tiled=True),
    )
    blk_rows, local_heads, _ = query_heads.shape
    tiles_here = blk_rows // TILE
    own_pair = (key_heads, value_heads)
    lower_list = []
    upper_list = []
    moving = own_pair
    for hop in range(2):
        moving = passed_along((moving[0], moving[1]), "blk", 1)
        lower_list.append(moving)
    moving = own_pair
    for hop in range(2):
        moving = passed_along((moving[0], moving[1]), "blk", -1)
        upper_list.append(moving)
    blocks = [lower_list[1], lower_list[0], own_pair, upper_list[0], upper_list[1]]
    key_window = jnp.concatenate([pair[0] for pair in blocks], axis=0).reshape(
        5 * tiles_here, TILE, local_heads, HDIM
    )
    value_window = jnp.concatenate([pair[1] for pair in blocks], axis=0).reshape(
        5 * tiles_here, TILE, local_heads, HDIM
    )
    first_tile = (position - 2) * tiles_here
    listed = lax.dynamic_slice_in_dim(kv_tiles, position * tiles_here, tiles_here, 0)
    own_frames = lax.dynamic_slice_in_dim(tile_frame, position * tiles_here, tiles_here, 0)
    frame_gap = jnp.abs(own_frames[:, None] - jnp.take(tile_frame, listed, axis=0)).astype(
        jnp.float32
    )
    window_index = listed - first_tile
    query_blocks = query_heads.reshape(tiles_here, TILE, local_heads, HDIM)
    win_count = listed.shape[1]

    def one_tile(operands):
        query_tile, indices, gaps = operands
        near_keys = jnp.take(key_window, indices, axis=0).reshape(
            win_count * TILE, local_heads, HDIM
        )
        near_values = jnp.take(value_window, indices, axis=0).reshape(
            win_count * TILE, local_heads, HDIM
        )
        score = jnp.einsum(
            "qhd,khd->hqk", query_tile, near_keys, preferred_element_type=jnp.float32
        ) * HDIM ** (-0.5)
        penalty = slopes[:, None] * gaps[None, :]
        score = (
            score.reshape(local_heads, TILE, win_count, TILE) - penalty[:, None, :, None]
        ).reshape(local_heads, TILE, win_count * TILE)
        weight = jnp.exp(score - jnp.max(score, axis=-1, keepdims=True))
        total = jnp.sum(weight, axis=-1)
        summed = jnp.einsum(
            "hqk,khd->qhd",
            weight.astype(jnp.bfloat16),
            near_values,
            preferred_element_type=jnp.float32,
        )
        return (summed / jnp.transpose(total)[:, :, None]).astype(jnp.bfloat16)

    attended = lax.map(one_tile, (query_blocks, window_index, frame_gap)).reshape(
        blk_rows, local_heads * HDIM
    )
    full_columns = lax.all_gather(out_weight, "blk", axis=1, tiled=True)
    mixed = lax.psum_scatter(
        jnp.dot(attended, full_columns, preferred_element_type=jnp.float32).astype(jnp.bfloat16),
        "head",
        scatter_dimension=0,
        tiled=True,
    )
    return mixed[None]


def solution(mesh):
    placed = (
        P("head", "blk", None),
        P("head", "blk", None),
        P("head", "blk", None),
        P(),
        P(),
        P("head"),
        P("head", "blk"),
        P(),
        P(),
    )
    return jax.shard_map(
        shards, mesh=mesh, in_specs=placed, out_specs=P("head", "blk", None), check_vma=False
    )
```

profile of v0, /device:TPU:24, one launch (start us, length us, event | category | flops | bytes accessed | tf_op | source)
XLA Modules:
  0.0 907.7 jit_solution(16256751041575797301)
XLA Ops:
  6.5 0.7 all-gather.2.cloned.1.call-update
  7.3 6.3 copy.28
  13.5 3.0 multiply_reduce_fusion
  16.6 4.5 multiply_convert_fusion
  21.1 5.5 all-to-all-start.2
  26.6 6.3 copy.24
  32.9 39.0 %all-to-all-done.2 = bf16[384,40,128]{0,2,1:T(8,128)(2,1)} async-done(((bf16[384,40,128]{0,2,1:T(8,128)(2,1)}), bf16[384,40,128]{0,2,1:T(8,128)(2,1)}, u32[]{:S(2)}, u32[]{:S(2)}) %all-to-all-start.2) | async-done | bytes 3932192 | tf_op jit(solution)/shard_map/all_to_all | solution.py:35
  72.0 5.5 all-to-all-start
  77.5 6.3 copy.30
  83.8 1.9 collective-permute-start.4
  85.7 4.5 collective-permute-start.6
  90.3 31.7 %all-to-all-done = bf16[384,40,128]{0,2,1:T(8,128)(2,1)} async-done(((bf16[384,40,128]{0,2,1:T(8,128)(2,1)}), bf16[384,40,128]{0,2,1:T(8,128)(2,1)}, u32[]{:S(2)}, u32[]{:S(2)}) %all-to-all-start) | async-done | bytes 3932192 | tf_op jit(solution)/shard_map/all_to_all | solution.py:36
  122.0 6.3 copy.26
  128.4 1.9 collective-permute-start
  130.3 4.5 collective-permute-start.2
  134.8 48.8 %collective-permute-done.4 = bf16[768,20,128]{2,0,1:T(8,128)(2,1)} collective-permute-done((bf16[768,20,128]{2,0,1:T(8,128)(2,1)}, bf16[768,20,128]{2,0,1:T(8,128)(2,1)}, u32[]{:S(2)}, u32[]{:S(2)}) %collective-permute-start.4) | collective-permute-done | bytes 3932192 | tf_op jit(solution)/shard_map/ppermute | solution.py:14
  183.6 1.9 collective-permute-start.5
  185.6 4.5 collective-permute-start.7
  190.1 35.7 %collective-permute-done = bf16[768,20,128]{2,0,1:T(8,128)(2,1)} collective-permute-done((bf16[768,20,128]{2,0,1:T(8,128)(2,1)}, bf16[768,20,128]{2,0,1:T(8,128)(2,1)}, u32[]{:S(2)}, u32[]{:S(2)}) %collective-permute-start) | collective-permute-done | bytes 3932192 | tf_op jit(solution)/shard_map/ppermute | solution.py:14
  225.8 130.0 %collective-permute-start.1 = (bf16[768,20,128]{2,0,1:T(8,128)(2,1)}, bf16[768,20,128]{2,0,1:T(8,128)(2,1)}, u32[]{:S(2)}, u32[]{:S(2)}) collective-permute-start(bf16[768,20,128]{2,0,1:T(8,128)(2,1)} %collective-permute-done), channel_id=1, source_target_pairs={{0,1},{1,2},{2,3},{3,4},{4,5},{5,6},{6,7},{7,8},{8,9},{9,10},{10,1... | collective-permute-start | bytes 11796488 | tf_op jit(solution)/shard_map/ppermute | solution.py:14
  355.8 1.9 collective-permute-start.3
  357.8 3.1 convert_bitcast_fusion
  360.9 1.6 copy.38
  362.5 0.5 copy-done.3
  363.0 0.8 fusion.23
  363.8 3.6 fusion.25
  367.4 5.5 all-to-all-start.1
  372.9 0.2 reduce-scatter.2.cloned.1.call-start
  373.2 0.1 constant_dynamic-slice_fusion.2
  373.3 0.1 copy.36
  373.4 0.1 reshape.133
  373.5 0.6 gather_fusion.2
  374.2 0.1 reshape.132
  374.4 2.6 constant_dynamic-update-slice_fusion.9
  376.9 2.7 constant_dynamic-update-slice_fusion.8
  379.7 0.5 constant_dynamic-update-slice_fusion.7
  380.2 2.7 constant_dynamic-update-slice_fusion.6
  383.0 2.7 constant_dynamic-update-slice_fusion.5
  385.7 50.6 %copy.32 = bf16[10,384,20,128]{3,2,1,0:T(8,128)(2,1)} copy(bf16[10,384,20,128]{3,1,0,2:T(8,128)(2,1)S(1)} %bitcast.81) | data formatting | bytes 39321600 | tf_op jit(solution)/shard_map/while | solution.py:93
  436.4 2.5 constant_dynamic-update-slice_fusion.4
  438.9 2.7 constant_dynamic-update-slice_fusion.3
  441.7 0.5 constant_dynamic-update-slice_fusion.2
  442.2 2.7 constant_dynamic-update-slice_fusion.1
  444.9 2.7 constant_dynamic-update-slice_fusion
  447.7 50.6 %copy.31 = bf16[10,384,20,128]{3,2,1,0:T(8,128)(2,1)} copy(bf16[10,384,20,128]{3,1,0,2:T(8,128)(2,1)S(1)} %bitcast.82) | data formatting | bytes 39321600 | tf_op jit(solution)/shard_map/while | solution.py:93
  498.4 213.2 %while.10 = (s32[]{:T(128)}, bf16[2,384,20,128]{1,3,2,0:T(8,128)(2,1)}, s32[2,4]{1,0:T(2,128)S(1)}, bf16[10,384,20,128]{3,2,1,0:T(8,128)(2,1)}, bf16[2,384,20,12...) while((s32[]{:T(128)}, ...), condition=%wide.region_5.7_spmd, body=%wide.region_2.6_spmd.sunk | while | flops 6179375104 | bytes 228495312 | solution.py:93
  498.6 12.8 %gather_fusion = bf16[4,384,20,128]{3,2,1,0:T(8,128)(2,1)} fusion(bf16[10,384,20,128]{3,2,1,0:T(8,128)(2,1)} %get-tuple-element.165, s32[1024]{0:T(1024)S(1)} %pad_clamp_fusion.3), kind=kCustom, calls=%fused_computation.clone.clone.1 | custom fusion | bytes 15728656 | tf_op jit(solution)/shard_map/while/body/eval_jaxpr/jit(_take)/gather | solution.py:73
  511.4 12.8 %gather_fusion.1 = bf16[4,384,20,128]{3,2,1,0:T(8,128)(2,1)} fusion(bf16[10,384,20,128]{3,2,1,0:T(8,128)(2,1)} %get-tuple-element.167, s32[1024]{0:T(1024)S(1)} %pad_clamp_fusion.3), kind=kCustom, calls=%fused_computation.1.clone.clone.1 | custom fusion | bytes 15728656 | tf_op jit(solution)/shard_map/while/body/eval_jaxpr/jit(_take)/gather | solution.py:70
  524.1 14.9 %broadcast_select_fusion.3 = (bf16[4,384,20,128]{3,2,1,0:T(8,128)(2,1)}, bf16[4,384,20,128]{3,2,1,0:T(8,128)(2,1)}) fusion(bf16[4,384,20,128]{3,2,1,0:T(8,128)(2,1)} %gather_fusion, pred[4]{0:T(512)(128)(4,1)S(1)} %get-tuple-element.137, bf16[4,384,20,128]{3,2,1,0:T(8,128)(2,1)} %gather_fusion.1), kind=kLoop, calls=%fused_computation.10.clone.1 | loop fusion | flops 7864320 | bytes 31457284 | tf_op jit(solution)/shard_map/while/body/eval_jaxpr/jit(_take)/select_n | solution.py:73
  539.2 0.1 sub.109
  539.3 20.6 %fusion.37 = (f32[20,384]{1,0:T(8,128)S(1)}, f32[20,384,1536]{2,1,0:T(8,128)}) fusion(f32[20,1536]{1,0:T(8,128)S(1)} %bitcast.76, bf16[1536,20,128]{2,1,0:T(8,128)(2,1)} %bitcast.74, bf16[2,384,20,128]{3,1,2,0:T(8,128)(2,1)} %get-tuple-element.166, s32[]{:T(128)} %get-tuple-element.152), kind=kOutput, calls=%fused_computation.5.clone.1 | convolution fusion | flops 3055280640 | bytes 58743296 | tf_op jit(solution)/shard_map/while/body/eval_jaxpr/qhd,khd->hqk/dot_general | solution.py:76
  559.9 20.4 %fusion.38 = f32[20,384]{1,0:T(8,128)S(1)} fusion(f32[20,384,1536]{2,1,0:T(8,128)} %get-tuple-element.139, f32[20,384]{1,0:T(8,128)S(1)} %get-tuple-element.140, f32[20,1536]{1,0:T(8,128)S(1)} %bitcast.77), kind=kLoop, calls=%fused_computation.6.clone.1 | loop fusion | flops 47178240 | bytes 47370240 | tf_op jit(solution)/shard_map/while/body/eval_jaxpr/reduce_sum | solution.py:84
  580.3 24.7 %bitcast_dynamic-update-slice_fusion.2 = bf16[2,384,20,128]{1,3,2,0:T(8,128)(2,1)} fusion(bf16[2,384,20,128]{1,3,2,0:T(8,128)(2,1)} %get-tuple-element.153, s32[]{:T(128)} %get-tuple-element.152, f32[384,20]{0,1:T(8,128)S(1)} %bitcast.93, f32[20,384,1536]{2,1,0:T(8,128)} %get-tuple-element.139, f32[20,384]{1,0:T(8,128)S(1)} %get-tuple-element.140, ...), kind=kOutput, calls=%fused_computation.16.clone.1 | convolution fusion | flops 3069050880 | bytes 58774016 | tf_op jit(solution)/shard_map/while/body/eval_jaxpr/hqk,khd->qhd/dot_general | solution.py:85
  605.0 12.8 %gather_fusion = bf16[4,384,20,128]{3,2,1,0:T(8,128)(2,1)} fusion(bf16[10,384,20,128]{3,2,1,0:T(8,128)(2,1)} %get-tuple-element.165, s32[1024]{0:T(1024)S(1)} %pad_clamp_fusion.3), kind=kCustom, calls=%fused_computation.clone.clone.1 | custom fusion | bytes 15728656 | tf_op jit(solution)/shard_map/while/body/eval_jaxpr/jit(_take)/gather | solution.py:73
  617.8 12.8 %gather_fusion.1 = bf16[4,384,20,128]{3,2,1,0:T(8,128)(2,1)} fusion(bf16[10,384,20,128]{3,2,1,0:T(8,128)(2,1)} %get-tuple-element.167, s32[1024]{0:T(1024)S(1)} %pad_clamp_fusion.3), kind=kCustom, calls=%fused_computation.1.clone.clone.1 | custom fusion | bytes 15728656 | tf_op jit(solution)/shard_map/while/body/eval_jaxpr/jit(_take)/gather | solution.py:70
  630.5 14.9 %broadcast_select_fusion.3 = (bf16[4,384,20,128]{3,2,1,0:T(8,128)(2,1)}, bf16[4,384,20,128]{3,2,1,0:T(8,128)(2,1)}) fusion(bf16[4,384,20,128]{3,2,1,0:T(8,128)(2,1)} %gather_fusion, pred[4]{0:T(512)(128)(4,1)S(1)} %get-tuple-element.137, bf16[4,384,20,128]{3,2,1,0:T(8,128)(2,1)} %gather_fusion.1), kind=kLoop, calls=%fused_computation.10.clone.1 | loop fusion | flops 7864320 | bytes 31457284 | tf_op jit(solution)/shard_map/while/body/eval_jaxpr/jit(_take)/select_n | solution.py:73
  645.6 0.1 sub.109
  645.7 20.6 %fusion.37 = (f32[20,384]{1,0:T(8,128)S(1)}, f32[20,384,1536]{2,1,0:T(8,128)}) fusion(f32[20,1536]{1,0:T(8,128)S(1)} %bitcast.76, bf16[1536,20,128]{2,1,0:T(8,128)(2,1)} %bitcast.74, bf16[2,384,20,128]{3,1,2,0:T(8,128)(2,1)} %get-tuple-element.166, s32[]{:T(128)} %get-tuple-element.152), kind=kOutput, calls=%fused_computation.5.clone.1 | convolution fusion | flops 3055280640 | bytes 58743296 | tf_op jit(solution)/shard_map/while/body/eval_jaxpr/qhd,khd->hqk/dot_general | solution.py:76
  666.3 20.4 %fusion.38 = f32[20,384]{1,0:T(8,128)S(1)} fusion(f32[20,384,1536]{2,1,0:T(8,128)} %get-tuple-element.139, f32[20,384]{1,0:T(8,128)S(1)} %get-tuple-element.140, f32[20,1536]{1,0:T(8,128)S(1)} %bitcast.77), kind=kLoop, calls=%fused_computation.6.clone.1 | loop fusion | flops 47178240 | bytes 47370240 | tf_op jit(solution)/shard_map/while/body/eval_jaxpr/reduce_sum | solution.py:84
  686.6 24.7 %bitcast_dynamic-update-slice_fusion.2 = bf16[2,384,20,128]{1,3,2,0:T(8,128)(2,1)} fusion(bf16[2,384,20,128]{1,3,2,0:T(8,128)(2,1)} %get-tuple-element.153, s32[]{:T(128)} %get-tuple-element.152, f32[384,20]{0,1:T(8,128)S(1)} %bitcast.93, f32[20,384,1536]{2,1,0:T(8,128)} %get-tuple-element.139, f32[20,384]{1,0:T(8,128)S(1)} %get-tuple-element.140, ...), kind=kOutput, calls=%fused_computation.16.clone.1 | convolution fusion | flops 3069050880 | bytes 58774016 | tf_op jit(solution)/shard_map/while/body/eval_jaxpr/hqk,khd->qhd/dot_general | solution.py:85
  711.6 6.2 copy.33
  717.8 2.6 copy.39
  720.4 26.6 %convolution_convert_fusion = bf16[768,5120]{1,0:T(8,128)(2,1)} fusion(bf16[768,2560]{0,1:T(8,128)(2,1)} %bitcast.92, bf16[2560,5120]{0,1:T(8,128)(2,1)} %all-gather.2.cloned.1.call-done), kind=kOutput, calls=%fused_computation.31 | convolution fusion | flops 20136591360 | bytes 38010880 | tf_op jit(solution)/shard_map/dot_general | solution.py:98
  747.0 153.4 %reduce-scatter.2.cloned.1.call-done = bf16[384,5120]{1,0:T(8,128)(2,1)} async-done(((bf16[768,5120]{1,0:T(8,128)(2,1)}), bf16[384,5120]{1,0:T(8,128)(2,1)}) %reduce-scatter.2.cloned.1.call-update) | async-done | bytes 3932176 | tf_op jit(solution)/shard_map/reduce_scatter | solution.py:97
  (46 shorter events, 0.5 us)
Async XLA Ops:
  6.5 366.7 %copy-start = (s32[32,4]{0,1:T(4,128)S(1)}, s32[32,4]{0,1:T(4,128)}, u32[]{:S(2)}) copy-start(s32[32,4]{0,1:T(4,128)} %param.20) | copy-start | bytes 1540
  6.5 10.0 %copy-start.6 = (f32[5120]{0:T(1024)S(1)}, f32[5120]{0:T(1024)}, u32[]{:S(2)}) copy-start(f32[5120]{0:T(1024)} %param.17) | copy-start | bytes 61444
  6.5 713.8 %all-gather.2.cloned.1.call-start = ((), (), s32[]{:S(2)}) async-start(), calls=%async_computation.4 | async-start | bytes 27852800 | tf_op jit(solution)/shard_map/all_gather | solution.py:96
  21.1 50.9 %all-to-all-start.2 = ((bf16[384,40,128]{0,2,1:T(8,128)(2,1)}), bf16[384,40,128]{0,2,1:T(8,128)(2,1)}, u32[]{:S(2)}, u32[]{:S(2)}) async-start(bf16[384,40,128]{0,2,1:T(8,128)(2,1)} %multiply_convert_fusion), calls=%async_computation.2 | async-start | bytes 7864320 | tf_op jit(solution)/shard_map/all_to_all | solution.py:35
  72.0 50.1 %all-to-all-start = ((bf16[384,40,128]{0,2,1:T(8,128)(2,1)}), bf16[384,40,128]{0,2,1:T(8,128)(2,1)}, u32[]{:S(2)}, u32[]{:S(2)}) async-start(bf16[384,40,128]{0,2,1:T(8,128)(2,1)} %bitcast.89), calls=%async_computation | async-start | bytes 7864320 | tf_op jit(solution)/shard_map/all_to_all | solution.py:36
  83.8 99.8 %collective-permute-start.4 = (bf16[768,20,128]{2,0,1:T(8,128)(2,1)}, bf16[768,20,128]{2,0,1:T(8,128)(2,1)}, u32[]{:S(2)}, u32[]{:S(2)}) collective-permute-start(bf16[768,20,128]{2,0,1:T(8,128)(2,1)} %bitcast.86), channel_id=1, source_target_pairs={{0,1},{1,2},{2,3},{3,4},{4,5},{5,6},{6,7},{7,8},{8,9},{9,10},{10,1... | collective-permute-start | bytes 11796488 | tf_op jit(solution)/shard_map/ppermute | solution.py:14
  85.7 99.8 %collective-permute-start.6 = (bf16[768,20,128]{2,0,1:T(8,128)(2,1)}, bf16[768,20,128]{2,0,1:T(8,128)(2,1)}, u32[]{:S(2)}, u32[]{:S(2)}) collective-permute-start(bf16[768,20,128]{2,0,1:T(8,128)(2,1)} %bitcast.87), channel_id=1, source_target_pairs={{1,0},{2,1},{3,2},{4,3},{5,4},{6,5},{7,6},{8,7},{9,8},{10,9},{11,1... | collective-permute-start | bytes 11796488 | tf_op jit(solution)/shard_map/ppermute | solution.py:14
  128.4 97.4 %collective-permute-start = (bf16[768,20,128]{2,0,1:T(8,128)(2,1)}, bf16[768,20,128]{2,0,1:T(8,128)(2,1)}, u32[]{:S(2)}, u32[]{:S(2)}) collective-permute-start(bf16[768,20,128]{2,0,1:T(8,128)(2,1)} %bitcast.83), channel_id=1, source_target_pairs={{0,1},{1,2},{2,3},{3,4},{4,5},{5,6},{6,7},{7,8},{8,9},{9,10},{10,1... | collective-permute-start | bytes 11796488 | tf_op jit(solution)/shard_map/ppermute | solution.py:14
  130.3 225.5 %collective-permute-start.2 = (bf16[768,20,128]{2,0,1:T(8,128)(2,1)}, bf16[768,20,128]{2,0,1:T(8,128)(2,1)}, u32[]{:S(2)}, u32[]{:S(2)}) collective-permute-start(bf16[768,20,128]{2,0,1:T(8,128)(2,1)} %bitcast.84), channel_id=1, source_target_pairs={{1,0},{2,1},{3,2},{4,3},{5,4},{6,5},{7,6},{8,7},{9,8},{10,9},{11,1... | collective-permute-start | bytes 11796488 | tf_op jit(solution)/shard_map/ppermute | solution.py:14
  183.6 190.7 %collective-permute-start.5 = (bf16[768,20,128]{2,0,1:T(8,128)(2,1)}, bf16[768,20,128]{2,0,1:T(8,128)(2,1)}, u32[]{:S(2)}, u32[]{:S(2)}) collective-permute-start(bf16[768,20,128]{2,0,1:T(8,128)(2,1)} %collective-permute-done.4), channel_id=1, source_target_pairs={{0,1},{1,2},{2,3},{3,4},{4,5},{5,6},{6,7},{7,8},{8,9},{9,10},{10,1... | collective-permute-start | bytes 11796488 | tf_op jit(solution)/shard_map/ppermute | solution.py:14
  185.6 197.4 %collective-permute-start.7 = (bf16[768,20,128]{2,0,1:T(8,128)(2,1)}, bf16[768,20,128]{2,0,1:T(8,128)(2,1)}, u32[]{:S(2)}, u32[]{:S(2)}) collective-permute-start(bf16[768,20,128]{2,0,1:T(8,128)(2,1)} %collective-permute-done.6), channel_id=1, source_target_pairs={{1,0},{2,1},{3,2},{4,3},{5,4},{6,5},{7,6},{8,7},{9,8},{10,9},{11,1... | collective-permute-start | bytes 11796488 | tf_op jit(solution)/shard_map/ppermute | solution.py:14
  225.8 210.6 %collective-permute-start.1 = (bf16[768,20,128]{2,0,1:T(8,128)(2,1)}, bf16[768,20,128]{2,0,1:T(8,128)(2,1)}, u32[]{:S(2)}, u32[]{:S(2)}) collective-permute-start(bf16[768,20,128]{2,0,1:T(8,128)(2,1)} %collective-permute-done), channel_id=1, source_target_pairs={{0,1},{1,2},{2,3},{3,4},{4,5},{5,6},{6,7},{7,8},{8,9},{9,10},{10,1... | collective-permute-start | bytes 11796488 | tf_op jit(solution)/shard_map/ppermute | solution.py:14
  355.8 89.1 %collective-permute-start.3 = (bf16[768,20,128]{2,0,1:T(8,128)(2,1)}, bf16[768,20,128]{2,0,1:T(8,128)(2,1)}, u32[]{:S(2)}, u32[]{:S(2)}) collective-permute-start(bf16[768,20,128]{2,0,1:T(8,128)(2,1)} %collective-permute-done.2), channel_id=1, source_target_pairs={{1,0},{2,1},{3,2},{4,3},{5,4},{6,5},{7,6},{8,7},{9,8},{10,9},{11,1... | collective-permute-start | bytes 11796488 | tf_op jit(solution)/shard_map/ppermute | solution.py:14
  360.8 2.1 copy-start.3
  360.8 3.0 copy-start.7
  363.8 9.6 %copy-start.2 = (s32[32]{0:T(128)S(1)}, s32[32]{0:T(128)}, u32[]{:S(2)}) copy-start(s32[32]{0:T(128)} %param.21) | copy-start | bytes 388
  367.4 130.9 %all-to-all-start.1 = ((bf16[384,40,128]{2,0,1:T(8,128)(2,1)}), bf16[384,40,128]{2,0,1:T(8,128)(2,1)}, u32[]{:S(2)}, u32[]{:S(2)}) async-start(bf16[384,40,128]{2,0,1:T(8,128)(2,1)} %fusion.25), calls=%async_computation.1 | async-start | bytes 7864320 | tf_op jit(solution)/shard_map/all_to_all | solution.py:34
  372.9 527.4 %reduce-scatter.2.cloned.1.call-start = ((), (), s32[]{:S(2)}) async-start(), calls=%async_computation.5 | async-start | bytes 11796480 | tf_op jit(solution)/shard_map/reduce_scatter | solution.py:97
  374.3 5.4 copy-start.5
  436.3 5.3 copy-start.4
  447.7 50.7 %copy-start.8 = (f32[20]{0:T(128)S(1)}, f32[20]{0:T(128)}, u32[]{:S(2)}) copy-start(f32[20]{0:T(128)} %param.18) | copy-start | bytes 244
  720.4 180.0 %copy-start.1 = (s32[32,4]{0,1:T(4,128)S(1)}, s32[32,4]{0,1:T(4,128)}, u32[]{:S(2)}) copy-start(s32[32,4]{0,1:T(4,128)} %param.20) | copy-start | bytes 1540
Sparse Core Ops, SparseCore 0:
  9.0 328.0 all-gather.1
  747.1 153.2 reduce-scatter.1
where the time goes:
time: 918 us; the launch traced here: 908 us
  waiting for transfers between devices  309 us (34%)
  local copies, waits for them, and re-layouts  212 us (23%)
  starting transfers between devices  168 us (18%)
  matrix products  117 us (13%)
  other arithmetic  85.9 us (9%)
  between operations  14.2 us (2%)
    reduce_scatter x1, waiting for transfers between devices, shards(): lax.psum_scatter(jnp.dot(attended, full_columns, preferred_element_type=j...  153 us
    ppermute x8, starting transfers between devices, passed_along(): lax.ppermute(value, axis, [(source, source + steps) for source in range(i...  151 us
    while x3, local copies, waits for them, and re-layouts, shards(): lax.map(one_tile, (query_blocks, window_index, frame_gap))  107 us
    ppermute x8, waiting for transfers between devices, passed_along(): lax.ppermute(value, axis, [(source, source + steps) for source in range(i...  84.5 us
    dot_general x2, matrix products, one_tile(): jnp.einsum('hqk,khd->qhd', weight.astype(jnp.bfloat16), near_values, pref...  49.4 us
    dot_general x2, matrix products, one_tile(): jnp.einsum('qhd,khd->hqk', query_tile, near_keys, preferred_element_type=...  41.1 us
    reduce_sum x2, other arithmetic, one_tile(): total = jnp.sum(weight, axis=-1)  40.7 us
    all_to_all x1, waiting for transfers between devices, shards(): lax.all_to_all(by_head[1], 'head', split_axis=1, concat_axis=0, tiled=True)  39 us
  transfers between devices with their start and end apart: 13, of which 5 were waited for; matrix products, arithmetic and copies ran while one was open for 43% of the time, Pallas kernels for 0%

commit v1 on v0

v1 whole, which is shorter than its diff:
```python
import math

import jax
import jax.numpy as jnp
from jax import lax
from jax.experimental import pallas as pl
from jax.experimental.pallas import tpu as pltpu
from jax.sharding import PartitionSpec as P

HDIM = 128
TILE = 384
REACH = 3
LOG2E = math.log2(math.e)
CHUNKS = 4


def shifted(value, axis, steps):
    count = lax.axis_size(axis)
    initial, last = (max(0, -steps), min(count, count - steps))
    return lax.ppermute(value, axis, [(source, source + steps) for source in range(initial, last)])


def rms_norm(rows, gain):
    floats = rows.astype(jnp.float32)
    factor = lax.rsqrt(jnp.mean(floats * floats, axis=-1, keepdims=True) + 1e-06)
    return (floats * factor * gain).astype(jnp.bfloat16)


def attend_kernel(tiles, wins, parts, index_ref, penalty_ref, *refs):
    q_ref = refs[0]
    key_refs = refs[1 : 1 + parts]
    value_refs = refs[1 + parts : 1 + 2 * parts]
    out_ref, key_window, value_window = refs[1 + 2 * parts :]
    head = pl.program_id(0)
    for window, blocks in ((key_window, key_refs), (value_window, value_refs)):
        at = 0
        for block in blocks:
            for tile in range(block.shape[0] // TILE):
                window[at] = block[tile * TILE : (tile + 1) * TILE, :]
                at += 1
    for tile in range(tiles):
        query = q_ref[tile * TILE : (tile + 1) * TILE, :]
        scores = []
        largest = None
        for win in range(wins):
            near = key_window[index_ref[tile * wins + win]]
            score = lax.dot_general(
                query, near, (((1,), (1,)), ((), ())), preferred_element_type=jnp.float32
            )
            penalty = penalty_ref[(head * tiles + tile) * wins + win]
            top = jnp.max(score, axis=-1, keepdims=True) - penalty
            largest = top if largest is None else jnp.maximum(largest, top)
            scores.append((score, penalty))
        total = jnp.zeros((TILE, 1), jnp.float32)
        summed = jnp.zeros((TILE, HDIM), jnp.float32)
        for win, (score, penalty) in enumerate(scores):
            weight = jnp.exp2(score - (largest + penalty))
            total += jnp.sum(weight, axis=-1, keepdims=True)
            summed += jnp.dot(
                weight.astype(jnp.bfloat16),
                value_window[index_ref[tile * wins + win]],
                preferred_element_type=jnp.float32,
            )
        out_ref[tile * TILE : (tile + 1) * TILE, :] = (summed / total).astype(out_ref.dtype)


def attend(query, key_parts, value_parts, index, penalty):
    rows, width = query.shape
    heads, tiles, wins = width // HDIM, rows // TILE, index.shape[0] * TILE // rows
    window = sum(part.shape[0] for part in key_parts) // TILE

    def column(array):
        return pl.BlockSpec((array.shape[0], HDIM), lambda h, *_: (0, h))

    def body(*refs):
        attend_kernel(tiles, wins, len(key_parts), *refs)

    operands = (query, *key_parts, *value_parts)
    return pl.pallas_call(
        body,
        grid_spec=pltpu.PrefetchScalarGridSpec(
            num_scalar_prefetch=2,
            grid=(heads,),
            in_specs=[column(array) for array in operands],
            out_specs=column(query),
            scratch_shapes=[pltpu.VMEM((window, TILE, HDIM), jnp.bfloat16)] * 2,
        ),
        out_shape=jax.ShapeDtypeStruct(query.shape, jnp.bfloat16),
        compiler_params=pltpu.CompilerParams(vmem_limit_bytes=48 * 1024 * 1024),
        cost_estimate=pl.CostEstimate(
            flops=4 * rows * wins * TILE * width,
            bytes_accessed=2 * sum(array.size for array in operands) + 2 * query.size,
            transcendentals=rows * wins * TILE * heads,
        ),
    )(index, penalty, *operands)


def halo(own, tiles):
    near = min(REACH, tiles)
    far = REACH - near
    last = own.shape[0]
    lower, upper = [], []
    if far:
        lower.append(shifted(own[last - far * TILE :], "blk", 2))
        upper.append(shifted(own[: far * TILE], "blk", -2))
    lower.append(shifted(own[last - near * TILE :], "blk", 1))
    upper.insert(0, shifted(own[: near * TILE], "blk", -1))
    return [*lower, own, *upper]


def shards(queries, keys, values, q_gain, k_gain, slopes, out_weight, kv_tiles, tile_frame):
    groups = lax.axis_size("head")
    position, group = lax.axis_index("blk"), lax.axis_index("head")

    def to_heads(rows):
        return lax.all_to_all(rows, "head", split_axis=1, concat_axis=0, tiled=True)

    full_columns = lax.all_gather(out_weight, "blk", axis=1, tiled=True)
    value_own = to_heads(values[0])
    key_own = to_heads(rms_norm(keys[0], k_gain))
    query_own = to_heads(rms_norm(queries[0], q_gain * (LOG2E * HDIM ** (-0.5))))
    tiles = query_own.shape[0] // TILE
    key_parts, value_parts = halo(key_own, tiles), halo(value_own, tiles)

    listed = lax.dynamic_slice_in_dim(kv_tiles, position * tiles, tiles, 0)
    own_frames = lax.dynamic_slice_in_dim(tile_frame, position * tiles, tiles, 0)
    gap = jnp.abs(own_frames[:, None] - jnp.take(tile_frame, listed, axis=0)).astype(jnp.float32)
    penalty = (slopes * LOG2E)[:, None] * gap.reshape(1, -1)
    index = (listed - (position * tiles - REACH)).reshape(-1)
    attended = attend(query_own, key_parts, value_parts, index, penalty.reshape(-1))

    rows = attended.shape[0] // groups
    width = full_columns.shape[1] // CHUNKS

    def partial(owner, chunk):
        return jnp.dot(
            lax.dynamic_slice_in_dim(attended, owner * rows, rows, 0),
            full_columns[:, chunk * width : (chunk + 1) * width],
            preferred_element_type=jnp.float32,
        ).astype(jnp.bfloat16)

    arrived = []
    for chunk in range(CHUNKS):
        arrived.append(
            [
                lax.ppermute(
                    partial(lax.rem(group + step, groups), chunk),
                    "head",
                    [(source, (source + step) % groups) for source in range(groups)],
                )
                for step in range(1, groups)
            ]
        )
    mixed = []
    for chunk in range(CHUNKS):
        floats = partial(group, chunk).astype(jnp.float32)
        for term in arrived[chunk]:
            floats = floats + term.astype(jnp.float32)
        mixed.append(floats.astype(jnp.bfloat16))
    return jnp.concatenate(mixed, axis=1)[None]


def solution(mesh):
    placed = (
        P("head", "blk", None),
        P("head", "blk", None),
        P("head", "blk", None),
        P(),
        P(),
        P("head"),
        P("head", "blk"),
        P(),
        P(),
    )
    return jax.shard_map(
        shards, mesh=mesh, in_specs=placed, out_specs=P("head", "blk", None), check_vma=False
    )
```

time: 918 us -> 618 us (0.67)
  local copies, waits for them, and re-layouts: 212 us -> 46.4 us
  starting transfers between devices: 168 us -> 40.5 us
  waiting for transfers between devices: 309 us -> 398 us
  matrix products: 117 us -> 45.7 us
  other arithmetic: 85.9 us -> 21.7 us
  Pallas kernels: 0 us -> 51.2 us
    ppermute x8 -> x12, waiting for transfers between devices: 84.5 us -> 292 us  [the longest x8 264 us: shifted(): lax.ppermute(value, axis, [(source, source + steps) for source in range(i...]
    reduce_scatter x1 -> x0, waiting for transfers between devices: 153 us -> none  [shards(): lax.psum_scatter(jnp.dot(attended, full_columns, preferred_element_type=j...]
    ppermute x8 -> x12, starting transfers between devices: 151 us -> 23.8 us  [the longest x8 19.7 us: shifted(): lax.ppermute(value, axis, [(source, source + steps) for source in range(i...]
    while x7 -> x0, local copies, waits for them, and re-layouts: 108 us -> none  [the longest x3 107 us: shards(): lax.map(one_tile, (query_blocks, window_index, frame_gap))]
    dot_general x5 -> x8, matrix products: 117 us -> 45.7 us  [partial(): jnp.dot(lax.dynamic_slice_in_dim(attended, owner * rows, rows, 0), full_c...]
    pallas_call x0 -> x1, Pallas kernels: none -> 51.2 us  [attend(): pl.pallas_call(body, grid_spec=pltpu.PrefetchScalarGridSpec(num_scalar_pr...]
    gather x4 -> x0, local copies, waits for them, and re-layouts: 51.1 us -> none  [the longest x2 25.6 us: one_tile(): jnp.take(value_window, indices, axis=0)]
    reduce_sum x2 -> x0, other arithmetic: 40.7 us -> none  [one_tile(): total = jnp.sum(weight, axis=-1)]
  transfers between devices with their start and end apart: 13 -> 16, of which waited for: 5 -> 10; matrix products, arithmetic and copies ran while one was open for 43% -> 16% of each run, Pallas kernels for 0% -> 8%
where the time goes in v1:
time: 618 us; the launch traced here: 617 us
  waiting for transfers between devices  398 us (64%)
  Pallas kernels  51.2 us (8%)
  local copies, waits for them, and re-layouts  46.4 us (8%)
  matrix products  45.7 us (7%)
  starting transfers between devices  40.5 us (7%)
  other arithmetic  21.7 us (4%)
  between operations  13.6 us (2%)
    ppermute x8, waiting for transfers between devices, shifted(): lax.ppermute(value, axis, [(source, source + steps) for source in range(i...  264 us
    all_to_all x3, waiting for transfers between devices, to_heads(): return lax.all_to_all(rows, 'head', split_axis=1, concat_axis=0, tiled=True)  105 us
    pallas_call x1, Pallas kernels, attend(): pl.pallas_call(body, grid_spec=pltpu.PrefetchScalarGridSpec(num_scalar_pr...  51.2 us
    dot_general x8, matrix products, partial(): jnp.dot(lax.dynamic_slice_in_dim(attended, owner * rows, rows, 0), full_c...  45.7 us
    ppermute x4, waiting for transfers between devices, shards(): lax.ppermute(partial(lax.rem(group + step, groups), chunk), 'head', [(sou...  28 us
    ppermute x8, starting transfers between devices, shifted(): lax.ppermute(value, axis, [(source, source + steps) for source in range(i...  19.7 us
    convert_element_type x2, local copies, waits for them, and re-layouts, rms_norm(): floats = rows.astype(jnp.float32)  17.3 us
    all_to_all x3, starting transfers between devices, to_heads(): return lax.all_to_all(rows, 'head', split_axis=1, concat_axis=0, tiled=True)  16.7 us
  transfers between devices with their start and end apart: 16, of which 10 were waited for; matrix products, arithmetic and copies ran while one was open for 16% of the time, Pallas kernels for 8%

profile of v1, /device:TPU:24, one launch (start us, length us, event | category | flops | bytes accessed | tf_op | source)
XLA Modules:
  0.0 616.7 jit_solution(13501920259662945218)
XLA Ops:
  6.5 0.7 all-gather.2.cloned.1.call-update
  7.3 6.3 %copy.14 = bf16[1,384,5120]{1,2,0:T(8,128)(2,1)} copy(bf16[1,384,5120]{2,1,0:T(8,128)(2,1)} %param.10) | data formatting | bytes 7864320 | tf_op args[1]
  13.5 6.8 %copy.15 = f32[384,2,2560]{2,0,1:T(8,128)} copy(bf16[384,2,2560]{0,2,1:T(8,128)(2,1)} %bitcast.22) | data formatting | bytes 11796480 | tf_op jit(solution)/shard_map/convert_element_type | solution.py:24
  20.3 3.0 multiply_reduce_fusion
  23.4 6.6 %multiply_convert_fusion = bf16[384,2,2560]{2,0,1:T(8,128)(2,1)} fusion(f32[384,2,2560]{2,0,1:T(8,128)} %copy.15, f32[2,2560]{1,0:T(2,128)S(1)} %mul.108, f32[384]{0:T(512)S(1)} %add_rsqrt_fusion), kind=kLoop, calls=%fused_computation.4 | loop fusion | flops 5898240 | bytes 11818496 | tf_op jit(solution)/shard_map/convert_element_type | solution.py:26
  29.9 5.6 all-to-all-start.1
  35.5 6.3 %copy.16 = bf16[1,384,5120]{1,2,0:T(8,128)(2,1)} copy(bf16[1,384,5120]{2,1,0:T(8,128)(2,1)} %param.11) | data formatting | bytes 7864320 | tf_op args[2]
  41.8 6.4 %copy.17 = bf16[384,2,2560]{2,0,1:T(8,128)(2,1)} copy(bf16[384,2,2560]{0,2,1:T(8,128)(2,1)} %bitcast.23) | data formatting | bytes 7864320 | tf_op jit(solution)/shard_map/all_to_all | solution.py:116
  48.2 32.3 %all-to-all-done.1 = bf16[384,2,2560]{2,0,1:T(8,128)(2,1)} async-done(((bf16[384,2,2560]{2,0,1:T(8,128)(2,1)}), bf16[384,2,2560]{2,0,1:T(8,128)(2,1)}, u32[]{:S(2)}, u32[]{:S(2)}) %all-to-all-start.1) | async-done | bytes 3932192 | tf_op jit(solution)/shard_map/all_to_all | solution.py:116
  80.4 5.5 all-to-all-start.2
  86.0 4.4 slice_bitcast_fusion.2
  90.3 3.0 collective-permute-start
  93.4 3.7 collective-permute-start.3
  97.1 1.9 collective-permute-start.1
  99.0 31.0 %all-to-all-done.2 = bf16[384,2,2560]{2,0,1:T(8,128)(2,1)} async-done(((bf16[384,2,2560]{2,0,1:T(8,128)(2,1)}), bf16[384,2,2560]{2,0,1:T(8,128)(2,1)}, u32[]{:S(2)}, u32[]{:S(2)}) %all-to-all-start.2) | async-done | bytes 3932192 | tf_op jit(solution)/shard_map/all_to_all | solution.py:116
  130.0 4.3 slice_bitcast_fusion
  134.3 3.0 collective-permute-start.4
  137.4 1.9 collective-permute-start.2
  139.3 41.8 %collective-permute-done.refs_3_ = bf16[384,2560]{1,0:T(8,128)(2,1)S(1)} collective-permute-done((bf16[384,2560]{1,0:T(8,128)(2,1)}, bf16[384,2560]{1,0:T(8,128)(2,1)S(1)}, u32[]{:S(2)}, u32[]{:S(2)}) %collective-permute-start) | collective-permute-done | bytes 1966112 | tf_op jit(solution)/shard_map/ppermute | solution.py:20
  181.1 2.0 collective-permute-start.5
  183.2 166.6 %collective-permute-done.3.refs_7_ = bf16[384,2560]{1,0:T(8,128)(2,1)} collective-permute-done((bf16[384,2560]{1,0:T(8,128)(2,1)}, bf16[384,2560]{1,0:T(8,128)(2,1)}, u32[]{:S(2)}, u32[]{:S(2)}) %collective-permute-start.3) | collective-permute-done | bytes 1966112 | tf_op jit(solution)/shard_map/ppermute | solution.py:20
  349.8 1.9 collective-permute-start.6
  351.7 10.6 %reshape.101 = f32[384,2,2560]{2,1,0:T(2,128)} reshape(bf16[1,384,5120]{2,1,0:T(8,128)(2,1)} %param.9) | data formatting | bytes 11796480 | tf_op jit(solution)/shard_map/convert_element_type | solution.py:24
  362.3 3.0 multiply_reduce_fusion.1
  365.3 6.8 %fusion.1 = bf16[384,2,2560]{2,0,1:T(8,128)(2,1)} fusion(f32[384,2,2560]{2,1,0:T(2,128)} %reshape.101, f32[2,2560]{1,0:T(2,128)S(1)} %mul.102, f32[384]{0:T(512)S(1)} %add_rsqrt_fusion.1), kind=kLoop, calls=%fused_computation.3 | loop fusion | flops 5898240 | bytes 11818496 | tf_op jit(solution)/shard_map/convert_element_type | solution.py:26
  372.1 5.6 all-to-all-start
  377.7 0.0 collective-permute-done.4.refs_8_
  377.7 2.1 collective-permute-start.7
  379.9 0.1 constant_dynamic-slice_fusion
  379.9 0.1 copy.18
  380.0 0.1 reshape.105
  380.1 0.1 dynamic_slice.9
  380.2 0.6 gather_fusion
  380.8 0.1 reshape.104
  380.9 0.1 abs_convert_fusion
  381.0 0.1 convert_element_type.99
  381.1 0.1 broadcast_multiply_fusion.1
  381.2 0.1 mul.96.refs_1_
  381.3 0.1 reshape.100.refs_0_
  381.3 42.1 %all-to-all-done = bf16[384,2,2560]{2,0,1:T(8,128)(2,1)} async-done(((bf16[384,2,2560]{2,0,1:T(8,128)(2,1)}), bf16[384,2,2560]{2,0,1:T(8,128)(2,1)}, u32[]{:S(2)}, u32[]{:S(2)}) %all-to-all-start) | async-done | bytes 3932192 | tf_op jit(solution)/shard_map/all_to_all | solution.py:116
  423.4 55.1 %collective-permute-done.7.refs_12_ = bf16[384,2560]{1,0:T(8,128)(2,1)} collective-permute-done((bf16[384,2560]{1,0:T(8,128)(2,1)}, bf16[384,2560]{1,0:T(8,128)(2,1)}, u32[]{:S(2)}, u32[]{:S(2)}) %collective-permute-start.7) | collective-permute-done | bytes 1966112 | tf_op jit(solution)/shard_map/ppermute | solution.py:20
  478.5 0.0 collective-permute-done.1.refs_4_
  478.6 0.0 collective-permute-done.2.refs_6_
  478.6 0.0 collective-permute-done.5.refs_9_
  478.6 51.2 %shard_map.91 = bf16[768,2560]{1,0:T(8,128)(2,1)} custom-call(s32[8]{0:T(128)S(1)} %reshape.100.refs_0_, f32[160]{0:T(256)S(1)} %mul.96.refs_1_, bf16[768,2560]{1,0:T(8,128)(2,1)} %bitcast.1.refs_2_, bf16[384,2560]{1,0:T(8,128)(2,1)S(1)} %collective-permute-done.refs_3_, bf16[768,2560]{1,0:T(8,128)(2,1)} %collective-permute-done.1.refs_4_, ...), custom_call_target="tpu_custom_call" | custom-call | flops 12079595520 | bytes 39321600 | tf_op jit(solution)/shard_map/pallas_call | solution.py:79
  529.8 0.0 all-gather.2.cloned.1.call-done
  529.8 6.3 %fusion.30 = bf16[384,1280]{1,0:T(8,128)(2,1)S(1)} fusion(bf16[2560,5120]{0,1:T(8,128)(2,1)} %all-gather.2.cloned.1.call-done, bf16[768,2560]{1,0:T(8,128)(2,1)} %shard_map.91, s32[]{:T(128)S(6)} %select_n.34), kind=kOutput, calls=%fused_computation.28 | convolution fusion | flops 2517073920 | bytes 9502724 | tf_op jit(solution)/shard_map/dot_general | solution.py:136
  536.1 1.5 collective-permute-start.8
  537.7 7.9 %fusion.45 = bf16[384,1280]{1,0:T(8,128)(2,1)} fusion(bf16[2560,5120]{0,1:T(8,128)(2,1)} %all-gather.2.cloned.1.call-done, bf16[768,2560]{1,0:T(8,128)(2,1)} %shard_map.91, s32[]{:T(128)S(6)} %select_n.34), kind=kOutput, calls=%fused_computation.33 | convolution fusion | flops 2517073920 | bytes 9502724 | tf_op jit(solution)/shard_map/dot_general | solution.py:136
  545.5 0.6 collective-permute-start.9
  546.1 5.3 fusion.60
  551.4 1.5 collective-permute-start.10
  552.8 5.2 fusion.75
  558.0 0.6 collective-permute-start.11
  558.6 2.2 collective-permute-done.8
  560.9 4.3 fusion.27
  565.2 15.6 %collective-permute-done.9 = bf16[384,1280]{1,0:T(8,128)(2,1)} collective-permute-done((bf16[384,1280]{1,0:T(8,128)(2,1)}, bf16[384,1280]{1,0:T(8,128)(2,1)}, u32[]{:S(2)}, u32[]{:S(2)}) %collective-permute-start.9) | collective-permute-done | bytes 983072 | tf_op jit(solution)/shard_map/ppermute | solution.py:146
  580.8 4.5 fusion.42
  585.3 0.0 copy-start.7
  585.3 6.0 collective-permute-done.10
  591.3 6.4 %fusion.57 = bf16[384,1280]{1,0:T(8,128)(2,1)S(1)} fusion(bf16[2560,5120]{0,1:T(8,128)(2,1)} %all-gather.2.cloned.1.call-done, bf16[384,1280]{1,0:T(8,128)(2,1)} %collective-permute-done.10, bf16[768,2560]{1,0:T(8,128)(2,1)} %shard_map.91, s32[]{:T(128)S(6)} %select_n.33), kind=kOutput, calls=%fused_computation.37 | convolution fusion | flops 2519040000 | bytes 10485764 | tf_op jit(solution)/shard_map/dot_general | solution.py:136
  597.7 4.2 collective-permute-done.11
  601.9 5.8 fusion.72
  607.7 2.2 maximum_bitcast_fusion
  (25 shorter events, 0.1 us)
Async XLA Ops:
  6.5 373.3 %copy-start = (s32[32,4]{0,1:T(4,128)S(1)}, s32[32,4]{0,1:T(4,128)}, u32[]{:S(2)}) copy-start(s32[32,4]{0,1:T(4,128)} %param.16) | copy-start | bytes 1540
  6.5 523.2 %all-gather.2.cloned.1.call-start = ((), (), s32[]{:S(2)}) async-start(), calls=%async_computation.3 | async-start | bytes 27852800 | tf_op jit(solution)/shard_map/all_gather | solution.py:118
  13.5 6.8 %copy-start.3 = (f32[5120]{0:T(1024)S(1)}, f32[5120]{0:T(1024)}, u32[]{:S(2)}) copy-start(f32[5120]{0:T(1024)} %param.13) | copy-start | bytes 61444
  29.9 50.5 %all-to-all-start.1 = ((bf16[384,2,2560]{2,0,1:T(8,128)(2,1)}), bf16[384,2,2560]{2,0,1:T(8,128)(2,1)}, u32[]{:S(2)}, u32[]{:S(2)}) async-start(bf16[384,2,2560]{2,0,1:T(8,128)(2,1)} %multiply_convert_fusion), calls=%async_computation.1 | async-start | bytes 7864320 | tf_op jit(solution)/shard_map/all_to_all | solution.py:116
  80.4 49.6 %all-to-all-start.2 = ((bf16[384,2,2560]{2,0,1:T(8,128)(2,1)}), bf16[384,2,2560]{2,0,1:T(8,128)(2,1)}, u32[]{:S(2)}, u32[]{:S(2)}) async-start(bf16[384,2,2560]{2,0,1:T(8,128)(2,1)} %copy.17), calls=%async_computation.2 | async-start | bytes 7864320 | tf_op jit(solution)/shard_map/all_to_all | solution.py:116
  90.3 90.8 %collective-permute-start = (bf16[384,2560]{1,0:T(8,128)(2,1)}, bf16[384,2560]{1,0:T(8,128)(2,1)S(1)}, u32[]{:S(2)}, u32[]{:S(2)}) collective-permute-start(bf16[384,2560]{1,0:T(8,128)(2,1)} %get-tuple-element.8), channel_id=1, source_target_pairs={{0,2},{1,3},{2,4},{3,5},{4,6},{5,7},{6,8},{7,9},{8,10},{9,11},{10,... | collective-permute-start | bytes 5898248 | tf_op jit(solution)/shard_map/ppermute | solution.py:20
  93.4 256.4 %collective-permute-start.3 = (bf16[384,2560]{1,0:T(8,128)(2,1)}, bf16[384,2560]{1,0:T(8,128)(2,1)}, u32[]{:S(2)}, u32[]{:S(2)}) collective-permute-start(bf16[384,2560]{1,0:T(8,128)(2,1)} %get-tuple-element.7), channel_id=1, source_target_pairs={{2,0},{3,1},{4,2},{5,3},{6,4},{7,5},{8,6},{9,7},{10,8},{11,9},{12,... | collective-permute-start | bytes 5898248 | tf_op jit(solution)/shard_map/ppermute | solution.py:20
  97.1 381.5 %collective-permute-start.1 = (bf16[768,2560]{1,0:T(8,128)(2,1)}, bf16[768,2560]{1,0:T(8,128)(2,1)}, u32[]{:S(2)}, u32[]{:S(2)}) collective-permute-start(bf16[768,2560]{1,0:T(8,128)(2,1)} %bitcast.5.refs_5_), channel_id=1, source_target_pairs={{0,1},{1,2},{2,3},{3,4},{4,5},{5,6},{6,7},{7,8},{8,9},{9,10},{10,1... | collective-permute-start | bytes 11796488 | tf_op jit(solution)/shard_map/ppermute | solution.py:20
  134.3 243.4 %collective-permute-start.4 = (bf16[384,2560]{1,0:T(8,128)(2,1)}, bf16[384,2560]{1,0:T(8,128)(2,1)}, u32[]{:S(2)}, u32[]{:S(2)}) collective-permute-start(bf16[384,2560]{1,0:T(8,128)(2,1)} %get-tuple-element.6), channel_id=1, source_target_pairs={{0,2},{1,3},{2,4},{3,5},{4,6},{5,7},{6,8},{7,9},{8,10},{9,11},{10,... | collective-permute-start | bytes 5898248 | tf_op jit(solution)/shard_map/ppermute | solution.py:20
  137.4 341.2 %collective-permute-start.2 = (bf16[768,2560]{1,0:T(8,128)(2,1)}, bf16[768,2560]{1,0:T(8,128)(2,1)}, u32[]{:S(2)}, u32[]{:S(2)}) collective-permute-start(bf16[768,2560]{1,0:T(8,128)(2,1)} %bitcast.5.refs_5_), channel_id=1, source_target_pairs={{1,0},{2,1},{3,2},{4,3},{5,4},{6,5},{7,6},{8,7},{9,8},{10,9},{11,1... | collective-permute-start | bytes 11796488 | tf_op jit(solution)/shard_map/ppermute | solution.py:20
  181.1 181.2 %copy-start.4 = (f32[5120]{0:T(1024)S(1)}, f32[5120]{0:T(1024)}, u32[]{:S(2)}) copy-start(f32[5120]{0:T(1024)} %param.12) | copy-start | bytes 61444
  181.1 297.4 %collective-permute-start.5 = (bf16[768,2560]{1,0:T(8,128)(2,1)}, bf16[768,2560]{1,0:T(8,128)(2,1)}, u32[]{:S(2)}, u32[]{:S(2)}) collective-permute-start(bf16[768,2560]{1,0:T(8,128)(2,1)} %bitcast.11.refs_10_), channel_id=1, source_target_pairs={{0,1},{1,2},{2,3},{3,4},{4,5},{5,6},{6,7},{7,8},{8,9},{9,10},{10,1... | collective-permute-start | bytes 11796488 | tf_op jit(solution)/shard_map/ppermute | solution.py:20
  349.8 128.8 %collective-permute-start.6 = (bf16[768,2560]{1,0:T(8,128)(2,1)}, bf16[768,2560]{1,0:T(8,128)(2,1)}, u32[]{:S(2)}, u32[]{:S(2)}) collective-permute-start(bf16[768,2560]{1,0:T(8,128)(2,1)} %bitcast.11.refs_10_), channel_id=1, source_target_pairs={{1,0},{2,1},{3,2},{4,3},{5,4},{6,5},{7,6},{8,7},{9,8},{10,9},{11,1... | collective-permute-start | bytes 11796488 | tf_op jit(solution)/shard_map/ppermute | solution.py:20
  372.1 8.0 %copy-start.2 = (s32[32]{0:T(128)S(1)}, s32[32]{0:T(128)}, u32[]{:S(2)}) copy-start(s32[32]{0:T(128)} %param.17) | copy-start | bytes 388
  372.1 9.0 %copy-start.6 = (f32[20]{0:T(128)S(1)}, f32[20]{0:T(128)}, u32[]{:S(2)}) copy-start(f32[20]{0:T(128)} %param.14) | copy-start | bytes 244
  372.1 51.4 %all-to-all-start = ((bf16[384,2,2560]{2,0,1:T(8,128)(2,1)}), bf16[384,2,2560]{2,0,1:T(8,128)(2,1)}, u32[]{:S(2)}, u32[]{:S(2)}) async-start(bf16[384,2,2560]{2,0,1:T(8,128)(2,1)} %fusion.1), calls=%async_computation | async-start | bytes 7864320 | tf_op jit(solution)/shard_map/all_to_all | solution.py:116
  377.7 100.8 %collective-permute-start.7 = (bf16[384,2560]{1,0:T(8,128)(2,1)}, bf16[384,2560]{1,0:T(8,128)(2,1)}, u32[]{:S(2)}, u32[]{:S(2)}) collective-permute-start(bf16[384,2560]{1,0:T(8,128)(2,1)} %get-tuple-element.5), channel_id=1, source_target_pairs={{2,0},{3,1},{4,2},{5,3},{6,4},{7,5},{8,6},{9,7},{10,8},{11,9},{12,... | collective-permute-start | bytes 5898248 | tf_op jit(solution)/shard_map/ppermute | solution.py:20
  529.8 16.3 %copy-start.5 = (bf16[2560,5120]{0,1:T(8,128)(2,1)S(1)}, bf16[2560,5120]{0,1:T(8,128)(2,1)}, u32[]{:S(2)}) copy-start(bf16[2560,5120]{0,1:T(8,128)(2,1)} %all-gather.2.cloned.1.call-done) | copy-start | bytes 78643200
  536.1 24.8 %collective-permute-start.8 = (bf16[384,1280]{1,0:T(8,128)(2,1)S(1)}, bf16[384,1280]{1,0:T(8,128)(2,1)S(1)}, u32[]{:S(2)}, u32[]{:S(2)}) collective-permute-start(bf16[384,1280]{1,0:T(8,128)(2,1)S(1)} %fusion.30), channel_id=1, source_target_pairs={{0,16},{16,0},{1,17},{17,1},{2,18},{18,2},{3,19},{19,3},{4,20},{20... | collective-permute-start | bytes 2949128 | tf_op jit(solution)/shard_map/ppermute | solution.py:146
  545.5 35.2 %collective-permute-start.9 = (bf16[384,1280]{1,0:T(8,128)(2,1)}, bf16[384,1280]{1,0:T(8,128)(2,1)}, u32[]{:S(2)}, u32[]{:S(2)}) collective-permute-start(bf16[384,1280]{1,0:T(8,128)(2,1)} %fusion.45), channel_id=1, source_target_pairs={{0,16},{16,0},{1,17},{17,1},{2,18},{18,2},{3,19},{19,3},{4,20},{20... | collective-permute-start | bytes 2949128 | tf_op jit(solution)/shard_map/ppermute | solution.py:146
  551.4 40.0 %collective-permute-start.10 = (bf16[384,1280]{1,0:T(8,128)(2,1)}, bf16[384,1280]{1,0:T(8,128)(2,1)}, u32[]{:S(2)}, u32[]{:S(2)}) collective-permute-start(bf16[384,1280]{1,0:T(8,128)(2,1)} %fusion.60), channel_id=1, source_target_pairs={{0,16},{16,0},{1,17},{17,1},{2,18},{18,2},{3,19},{19,3},{4,20},{20... | collective-permute-start | bytes 2949128 | tf_op jit(solution)/shard_map/ppermute | solution.py:146
  558.0 43.8 %collective-permute-start.11 = (bf16[384,1280]{1,0:T(8,128)(2,1)}, bf16[384,1280]{1,0:T(8,128)(2,1)}, u32[]{:S(2)}, u32[]{:S(2)}) collective-permute-start(bf16[384,1280]{1,0:T(8,128)(2,1)} %fusion.75), channel_id=1, source_target_pairs={{0,16},{16,0},{1,17},{17,1},{2,18},{18,2},{3,19},{19,3},{4,20},{20... | collective-permute-start | bytes 2949128 | tf_op jit(solution)/shard_map/ppermute | solution.py:146
  585.3 16.6 %copy-start.7 = (bf16[768,2560]{1,0:T(8,128)(2,1)S(1)}, bf16[768,2560]{1,0:T(8,128)(2,1)}, u32[]{:S(2)}) copy-start(bf16[768,2560]{1,0:T(8,128)(2,1)} %shard_map.91) | copy-start | bytes 11796484
  601.9 8.0 %copy-start.1 = (s32[32,4]{0,1:T(4,128)S(1)}, s32[32,4]{0,1:T(4,128)}, u32[]{:S(2)}) copy-start(s32[32,4]{0,1:T(4,128)} %param.16) | copy-start | bytes 1540
Sparse Core Ops, SparseCore 0:
  9.0 350.2 all-gather.1

commit v2 on v1

--- a/solution.py
+++ b/solution.py
@@ -12,6 +12,8 @@
 REACH = 3
 LOG2E = math.log2(math.e)
 CHUNKS = 4
+TEAM = 8
+STEP = 2
 
 
 def shifted(value, axis, steps):
@@ -32,14 +34,20 @@
     value_refs = refs[1 + parts : 1 + 2 * parts]
     out_ref, key_window, value_window = refs[1 + 2 * parts :]
     head = pl.program_id(0)
-    for window, blocks in ((key_window, key_refs), (value_window, value_refs)):
-        at = 0
-        for block in blocks:
-            for tile in range(block.shape[0] // TILE):
-                window[at] = block[tile * TILE : (tile + 1) * TILE, :]
-                at += 1
-    for tile in range(tiles):
-        query = q_ref[tile * TILE : (tile + 1) * TILE, :]
+    first = pl.program_id(1) * STEP
+
+    @pl.when(first == 0)
+    def _():
+        for window, blocks in ((key_window, key_refs), (value_window, value_refs)):
+            at = 0
+            for block in blocks:
+                for tile in range(block.shape[0] // TILE):
+                    window[at] = block[tile * TILE : (tile + 1) * TILE, :]
+                    at += 1
+
+    for step in range(STEP):
+        tile = first + step
+        query = q_ref[step * TILE : (step + 1) * TILE, :]
         scores = []
         largest = None
         for win in range(wins):
@@ -61,7 +69,7 @@
                 value_window[index_ref[tile * wins + win]],
                 preferred_element_type=jnp.float32,
             )
-        out_ref[tile * TILE : (tile + 1) * TILE, :] = (summed / total).astype(out_ref.dtype)
+        out_ref[step * TILE : (step + 1) * TILE, :] = (summed / total).astype(out_ref.dtype)
 
 
 def attend(query, key_parts, value_parts, index, penalty):
@@ -70,7 +78,9 @@
     window = sum(part.shape[0] for part in key_parts) // TILE
 
     def column(array):
-        return pl.BlockSpec((array.shape[0], HDIM), lambda h, *_: (0, h))
+        return pl.BlockSpec((array.shape[0], HDIM), lambda h, t, *_: (0, h))
+
+    stepped = pl.BlockSpec((STEP * TILE, HDIM), lambda h, t, *_: (t, h))
 
     def body(*refs):
         attend_kernel(tiles, wins, len(key_parts), *refs)
@@ -80,9 +90,9 @@
         body,
         grid_spec=pltpu.PrefetchScalarGridSpec(
             num_scalar_prefetch=2,
-            grid=(heads,),
-            in_specs=[column(array) for array in operands],
-            out_specs=column(query),
+            grid=(heads, tiles // STEP),
+            in_specs=[stepped, *(column(array) for array in operands[1:])],
+            out_specs=stepped,
             scratch_shapes=[pltpu.VMEM((window, TILE, HDIM), jnp.bfloat16)] * 2,
         ),
         out_shape=jax.ShapeDtypeStruct(query.shape, jnp.bfloat16),
@@ -95,39 +105,63 @@
     )(index, penalty, *operands)
 
 
-def halo(own, tiles):
-    near = min(REACH, tiles)
-    far = REACH - near
-    last = own.shape[0]
-    lower, upper = [], []
-    if far:
-        lower.append(shifted(own[last - far * TILE :], "blk", 2))
-        upper.append(shifted(own[: far * TILE], "blk", -2))
-    lower.append(shifted(own[last - near * TILE :], "blk", 1))
-    upper.insert(0, shifted(own[: near * TILE], "blk", -1))
-    return [*lower, own, *upper]
+def halo(own, hop):
+    reach = REACH * TILE
+    lower = shifted(own[own.shape[0] - reach :], "blk", hop)
+    upper = shifted(own[:reach], "blk", -hop)
+    return [lower, own, upper]
 
 
 def shards(queries, keys, values, q_gain, k_gain, slopes, out_weight, kv_tiles, tile_frame):
-    groups = lax.axis_size("head")
+    groups, blocks = lax.axis_size("head"), lax.axis_size("blk")
     position, group = lax.axis_index("blk"), lax.axis_index("head")
+    hop = TEAM // groups
+    member = lax.rem(position, hop)
+    teams = [
+        [head * blocks + first + inner for inner in range(hop) for head in range(groups)]
+        for first in range(0, blocks, hop)
+    ]
+    lines = [list(range(first, first + hop)) for first in range(0, blocks, hop)]
+    length, features = values.shape[1:]
+    narrow = features // TEAM
 
     def to_heads(rows):
-        return lax.all_to_all(rows, "head", split_axis=1, concat_axis=0, tiled=True)
+        parts = rows.reshape(length, groups, hop, narrow).transpose(2, 1, 0, 3)
+        parts = lax.all_to_all(
+            parts.reshape(TEAM, length, narrow),
+            ("head", "blk"),
+            split_axis=0,
+            concat_axis=0,
+            axis_index_groups=teams,
+            tiled=True,
+        )
+        return parts.reshape(TEAM * length, narrow)
 
     full_columns = lax.all_gather(out_weight, "blk", axis=1, tiled=True)
     value_own = to_heads(values[0])
     key_own = to_heads(rms_norm(keys[0], k_gain))
     query_own = to_heads(rms_norm(queries[0], q_gain * (LOG2E * HDIM ** (-0.5))))
     tiles = query_own.shape[0] // TILE
-    key_parts, value_parts = halo(key_own, tiles), halo(value_own, tiles)
-
-    listed = lax.dynamic_slice_in_dim(kv_tiles, position * tiles, tiles, 0)
-    own_frames = lax.dynamic_slice_in_dim(tile_frame, position * tiles, tiles, 0)
+    key_parts, value_parts = halo(key_own, hop), halo(value_own, hop)
+
+    start = position // hop * tiles
+    listed = lax.dynamic_slice_in_dim(kv_tiles, start, tiles, 0)
+    own_frames = lax.dynamic_slice_in_dim(tile_frame, start, tiles, 0)
     gap = jnp.abs(own_frames[:, None] - jnp.take(tile_frame, listed, axis=0)).astype(jnp.float32)
-    penalty = (slopes * LOG2E)[:, None] * gap.reshape(1, -1)
-    index = (listed - (position * tiles - REACH)).reshape(-1)
+    heads = narrow // HDIM
+    own_slopes = lax.dynamic_slice_in_dim(slopes, member * heads, heads, 0)
+    penalty = (own_slopes * LOG2E)[:, None] * gap.reshape(1, -1)
+    index = (listed - (start - REACH)).reshape(-1)
     attended = attend(query_own, key_parts, value_parts, index, penalty.reshape(-1))
+    attended = lax.all_to_all(
+        attended.reshape(hop, groups * length, narrow),
+        "blk",
+        split_axis=0,
+        concat_axis=0,
+        axis_index_groups=lines,
+        tiled=True,
+    )
+    attended = attended.transpose(1, 0, 2).reshape(groups * length, hop * narrow)
 
     rows = attended.shape[0] // groups
     width = full_columns.shape[1] // CHUNKS

time: 618 us -> 507 us (0.82)
  the two profiles are of different devices: /device:TPU:24 before, /device:TPU:18 now
where the time goes in v2:
time: 507 us; the launch traced here: 498 us
  waiting for transfers between devices  237 us (47%)
  starting transfers between devices  78.4 us (15%)
  local copies, waits for them, and re-layouts  51.1 us (10%)
  Pallas kernels  51.1 us (10%)
  matrix products  46.6 us (9%)
  other arithmetic  19.6 us (4%)
  between operations  13.8 us (3%)
    ppermute x4, waiting for transfers between devices, shifted(): lax.ppermute(value, axis, [(source, source + steps) for source in range(i...  85.2 us
    all_to_all x3, waiting for transfers between devices, to_heads(): lax.all_to_all(parts.reshape(TEAM, length, narrow), ('head', 'blk'), spli...  57.3 us
    ppermute x4, starting transfers between devices, shifted(): lax.ppermute(value, axis, [(source, source + steps) for source in range(i...  53.2 us
    pallas_call x1, Pallas kernels, attend(): pl.pallas_call(body, grid_spec=pltpu.PrefetchScalarGridSpec(num_scalar_pr...  51.1 us
    ppermute x4, waiting for transfers between devices, shards(): lax.ppermute(partial(lax.rem(group + step, groups), chunk), 'head', [(sou...  48.7 us
    dot_general x8, matrix products, partial(): jnp.dot(lax.dynamic_slice_in_dim(attended, owner * rows, rows, 0), full_c...  46.6 us
    all_to_all x1, waiting for transfers between devices, shards(): lax.all_to_all(attended.reshape(hop, groups * length, narrow), 'blk', spl...  45.4 us
    convert_element_type x2, local copies, waits for them, and re-layouts, rms_norm(): floats = rows.astype(jnp.float32)  17.8 us
  transfers between devices with their start and end apart: 13, of which 11 were waited for; matrix products, arithmetic and copies ran while one was open for 21% of the time, Pallas kernels for 10%

profile of v2, /device:TPU:18, one launch (start us, length us, event | category | flops | bytes accessed | tf_op | source)
XLA Modules:
  0.0 497.8 jit_solution(3033496929300540592)
XLA Ops:
  6.5 0.0 all-gather.2.cloned.1.call-start
  6.5 0.7 all-gather.2.cloned.1.call-update
  7.3 8.9 %reshape.126 = f32[384,2,4,640]{3,2,1,0:T(4,128)} reshape(bf16[1,384,5120]{2,1,0:T(8,128)(2,1)} %param.10) | data formatting | bytes 11796480 | tf_op jit(solution)/shard_map/convert_element_type | solution.py:26
  16.2 3.9 multiply_reduce_fusion
  20.1 5.1 %fusion.17 = bf16[4,2,384,640]{3,0,1,2:T(4,128)(2,1)S(1)} fusion(f32[384,2,4,640]{3,2,1,0:T(4,128)} %reshape.126, f32[2,4,640]{2,1,0:T(4,128)S(1)} %mul.110, f32[384]{0:T(512)S(1)} %add_rsqrt_fusion), kind=kLoop, calls=%fused_computation.22 | loop fusion | flops 5898240 | bytes 11818496 | tf_op jit(solution)/shard_map/transpose | solution.py:129
  25.2 2.4 copy.16
  27.6 5.0 all-to-all-start.1
  32.6 8.3 %reshape_squeeze.3 = bf16[384,2,4,640]{3,2,1,0:T(4,128)(2,1)} reshape(bf16[1,384,5120]{2,1,0:T(8,128)(2,1)} %param.11) | data formatting | bytes 7864320 | tf_op jit(solution)/shard_map/reshape;squeeze | solution.py:129
  40.9 4.8 copy.17
  45.7 31.9 %all-to-all-done.1 = bf16[8,384,640]{2,1,0:T(8,128)(2,1)} async-done(((bf16[8,384,640]{2,1,0:T(8,128)(2,1)}), bf16[8,384,640]{2,1,0:T(8,128)(2,1)}, u32[]{:S(2)}, u32[]{:S(2)}) %all-to-all-start.1) | async-done | bytes 3932192 | tf_op jit(solution)/shard_map/all_to_all | solution.py:130
  77.5 5.5 %all-to-all-start.2 = ((bf16[8,384,640]{2,1,0:T(8,128)(2,1)}), bf16[8,384,640]{2,1,0:T(8,128)(2,1)}, u32[]{:S(2)}, u32[]{:S(2)}) async-start(bf16[8,384,640]{2,1,0:T(8,128)(2,1)} %bitcast.22), calls=%async_computation.2 | async-start | bytes 7864320 | tf_op jit(solution)/shard_map/all_to_all | solution.py:130
  83.0 8.9 %reshape.125 = f32[384,2,4,640]{3,2,1,0:T(4,128)} reshape(bf16[1,384,5120]{2,1,0:T(8,128)(2,1)} %param.9) | data formatting | bytes 11796480 | tf_op jit(solution)/shard_map/convert_element_type | solution.py:26
  92.0 0.0 copy-done.4
  92.0 3.0 multiply_reduce_fusion.1
  95.1 5.1 %fusion.16 = bf16[4,2,384,640]{3,0,1,2:T(4,128)(2,1)S(1)} fusion(f32[384,2,4,640]{3,2,1,0:T(4,128)} %reshape.125, f32[2,4,640]{2,1,0:T(4,128)S(1)} %mul.104, f32[384]{0:T(512)S(1)} %add_rsqrt_fusion.1), kind=kLoop, calls=%fused_computation.21 | loop fusion | flops 5898240 | bytes 11818496 | tf_op jit(solution)/shard_map/transpose | solution.py:129
  100.1 2.4 copy.15
  102.6 25.4 %all-to-all-done.2 = bf16[8,384,640]{2,1,0:T(8,128)(2,1)} async-done(((bf16[8,384,640]{2,1,0:T(8,128)(2,1)}), bf16[8,384,640]{2,1,0:T(8,128)(2,1)}, u32[]{:S(2)}, u32[]{:S(2)}) %all-to-all-start.2) | async-done | bytes 3932192 | tf_op jit(solution)/shard_map/all_to_all | solution.py:130
  128.0 5.8 %all-to-all-start = ((bf16[8,384,640]{2,1,0:T(8,128)(2,1)}), bf16[8,384,640]{2,1,0:T(8,128)(2,1)}, u32[]{:S(2)}, u32[]{:S(2)}) async-start(bf16[8,384,640]{2,1,0:T(8,128)(2,1)} %bitcast.21), calls=%async_computation | async-start | bytes 7864320 | tf_op jit(solution)/shard_map/all_to_all | solution.py:130
  133.8 3.7 fusion.87
  137.5 45.4 %collective-permute-start = (bf16[1152,640]{1,0:T(8,128)(2,1)}, bf16[1152,640]{1,0:T(8,128)(2,1)S(1)}, u32[]{:S(2)}, u32[]{:S(2)}) collective-permute-start(bf16[1152,640]{1,0:T(8,128)(2,1)} %bitcast.5), channel_id=1, source_target_pairs={{0,4},{1,5},{2,6},{3,7},{4,8},{5,9},{6,10},{7,11},{8,12},{9,13},{1... | collective-permute-start | bytes 4423688 | tf_op jit(solution)/shard_map/ppermute | solution.py:22
  183.0 0.0 copy-start.6
  183.0 1.9 collective-permute-start.1
  184.9 3.9 fusion.86
  188.8 3.8 collective-permute-start.2
  192.6 2.0 collective-permute-start.3
  194.7 0.1 constant_dynamic-slice_fusion
  194.8 0.1 copy.19
  194.9 0.1 reshape.129
  195.0 0.0 copy-done.2
  195.0 0.1 dynamic_slice.23
  195.0 0.7 gather_fusion
  195.7 0.1 reshape.128
  195.8 0.1 abs_convert_fusion
  195.9 0.1 convert_element_type.99
  196.0 0.1 dynamic-slice_multiply_fusion
  196.1 0.1 broadcast_multiply_fusion.1
  196.1 0.1 mul.98.refs_1_
  196.2 0.1 reshape.116.refs_0_
  196.3 0.0 all-to-all-done
  196.3 29.0 %collective-permute-done.refs_3_ = bf16[1152,640]{1,0:T(8,128)(2,1)S(1)} collective-permute-done((bf16[1152,640]{1,0:T(8,128)(2,1)}, bf16[1152,640]{1,0:T(8,128)(2,1)S(1)}, u32[]{:S(2)}, u32[]{:S(2)}) %collective-permute-start) | collective-permute-done | bytes 1474592 | tf_op jit(solution)/shard_map/ppermute | solution.py:22
  225.3 5.9 %collective-permute-done.1.refs_5_ = bf16[1152,640]{1,0:T(8,128)(2,1)S(1)} collective-permute-done((bf16[1152,640]{1,0:T(8,128)(2,1)}, bf16[1152,640]{1,0:T(8,128)(2,1)S(1)}, u32[]{:S(2)}, u32[]{:S(2)}) %collective-permute-start.1) | collective-permute-done | bytes 1474592 | tf_op jit(solution)/shard_map/ppermute | solution.py:22
  231.2 34.1 %collective-permute-done.2.refs_6_ = bf16[1152,640]{1,0:T(8,128)(2,1)} collective-permute-done((bf16[1152,640]{1,0:T(8,128)(2,1)}, bf16[1152,640]{1,0:T(8,128)(2,1)}, u32[]{:S(2)}, u32[]{:S(2)}) %collective-permute-start.2) | collective-permute-done | bytes 1474592 | tf_op jit(solution)/shard_map/ppermute | solution.py:22
  265.3 16.2 %collective-permute-done.3.refs_8_ = bf16[1152,640]{1,0:T(8,128)(2,1)} collective-permute-done((bf16[1152,640]{1,0:T(8,128)(2,1)}, bf16[1152,640]{1,0:T(8,128)(2,1)}, u32[]{:S(2)}, u32[]{:S(2)}) %collective-permute-start.3) | collective-permute-done | bytes 1474592 | tf_op jit(solution)/shard_map/ppermute | solution.py:22
  281.5 51.1 %shard_map.91 = bf16[3072,640]{1,0:T(8,128)(2,1)} custom-call(s32[32]{0:T(128)S(1)} %reshape.116.refs_0_, f32[160]{0:T(256)S(1)} %mul.98.refs_1_, bf16[3072,640]{1,0:T(8,128)(2,1)} %bitcast.2.refs_2_, bf16[1152,640]{1,0:T(8,128)(2,1)S(1)} %collective-permute-done.refs_3_, bf16[3072,640]{1,0:T(8,128)(2,1)} %bitcast.6.refs_4_, ...), custom_call_target="tpu_custom_call" | custom-call | flops 12079595520 | bytes 21626880 | tf_op jit(solution)/shard_map/pallas_call | solution.py:89
  332.6 6.3 %copy.18 = bf16[4,768,640]{1,2,0:T(8,128)(2,1)} copy(bf16[4,768,640]{2,1,0:T(8,128)(2,1)} %bitcast.25) | data formatting | bytes 7864320 | tf_op jit(solution)/shard_map/reshape | solution.py:157
  338.9 4.8 all-to-all-start.3
  343.7 45.4 %all-to-all-done.3 = bf16[4,768,640]{1,2,0:T(8,128)(2,1)} async-done(((bf16[4,768,640]{1,2,0:T(8,128)(2,1)}), bf16[4,768,640]{1,2,0:T(8,128)(2,1)}, u32[]{:S(2)}, u32[]{:S(2)}) %all-to-all-start.3) | async-done | bytes 3932192 | tf_op jit(solution)/shard_map/all_to_all | solution.py:156
  389.2 6.4 %fusion.24 = bf16[384,1280]{1,0:T(8,128)(2,1)S(1)} fusion(bf16[2560,5120]{0,1:T(8,128)(2,1)} %all-gather.2.cloned.1.call-done, bf16[768,2560]{0,1:T(8,128)(2,1)} %bitcast.15, s32[]{:T(128)S(6)} %select_n.44), kind=kOutput, calls=%fused_computation.26 | convolution fusion | flops 2517073920 | bytes 9502724 | tf_op jit(solution)/shard_map/dot_general | solution.py:170
  395.5 0.5 collective-permute-start.4
  396.0 7.9 %fusion.33 = bf16[384,1280]{1,0:T(8,128)(2,1)} fusion(bf16[2560,5120]{0,1:T(8,128)(2,1)} %all-gather.2.cloned.1.call-done, bf16[768,2560]{0,1:T(8,128)(2,1)} %bitcast.15, s32[]{:T(128)S(6)} %select_n.44), kind=kOutput, calls=%fused_computation.29 | convolution fusion | flops 2517073920 | bytes 9502724 | tf_op jit(solution)/shard_map/dot_general | solution.py:170
  403.9 1.6 collective-permute-start.5
  405.5 5.3 %fusion.42 = bf16[384,1280]{1,0:T(8,128)(2,1)} fusion(bf16[2560,5120]{0,1:T(8,128)(2,1)S(1)} %copy-done.5, bf16[768,2560]{0,1:T(8,128)(2,1)} %bitcast.15, s32[]{:T(128)S(6)} %select_n.44), kind=kOutput, calls=%fused_computation.32 | convolution fusion | flops 2517073920 | bytes 9502724 | tf_op jit(solution)/shard_map/dot_general | solution.py:170
  410.8 0.4 collective-permute-start.6
  411.2 5.2 %fusion.51 = bf16[384,1280]{1,0:T(8,128)(2,1)} fusion(bf16[2560,5120]{0,1:T(8,128)(2,1)S(1)} %copy-done.5, bf16[768,2560]{0,1:T(8,128)(2,1)} %bitcast.15, s32[]{:T(128)S(6)} %select_n.44), kind=kOutput, calls=%fused_computation.35 | convolution fusion | flops 2517073920 | bytes 9502724 | tf_op jit(solution)/shard_map/dot_general | solution.py:170
  416.4 1.6 collective-permute-start.7
  418.0 2.2 collective-permute-done.4
  420.3 4.5 add_convert_fusion.3
  424.8 16.7 %collective-permute-done.5 = bf16[384,1280]{1,0:T(8,128)(2,1)} collective-permute-done((bf16[384,1280]{1,0:T(8,128)(2,1)}, bf16[384,1280]{1,0:T(8,128)(2,1)}, u32[]{:S(2)}, u32[]{:S(2)}) %collective-permute-start.5) | collective-permute-done | bytes 983072 | tf_op jit(solution)/shard_map/ppermute | solution.py:180
  441.4 4.5 add_convert_fusion.2
  446.0 16.5 %collective-permute-done.6 = bf16[384,1280]{1,0:T(8,128)(2,1)} collective-permute-done((bf16[384,1280]{1,0:T(8,128)(2,1)}, bf16[384,1280]{1,0:T(8,128)(2,1)}, u32[]{:S(2)}, u32[]{:S(2)}) %collective-permute-start.6) | collective-permute-done | bytes 983072 | tf_op jit(solution)/shard_map/ppermute | solution.py:180
  462.5 6.4 %add_convert_fusion.1 = bf16[384,1280]{1,0:T(8,128)(2,1)S(1)} fusion(bf16[384,1280]{1,0:T(8,128)(2,1)} %collective-permute-done.6, bf16[2560,5120]{0,1:T(8,128)(2,1)} %all-gather.2.cloned.1.call-done, bf16[768,2560]{0,1:T(8,128)(2,1)} %bitcast.15, s32[]{:T(128)S(6)} %select_n.43), kind=kOutput, calls=%fused_computation.37 | convolution fusion | flops 2519040000 | bytes 10485764 | tf_op jit(solution)/shard_map/dot_general | solution.py:170
  468.9 13.3 %collective-permute-done.7 = bf16[384,1280]{1,0:T(8,128)(2,1)} collective-permute-done((bf16[384,1280]{1,0:T(8,128)(2,1)}, bf16[384,1280]{1,0:T(8,128)(2,1)}, u32[]{:S(2)}, u32[]{:S(2)}) %collective-permute-start.7) | collective-permute-done | bytes 983072 | tf_op jit(solution)/shard_map/ppermute | solution.py:180
  482.2 6.4 %add_convert_fusion = bf16[384,1280]{1,0:T(8,128)(2,1)S(1)} fusion(bf16[384,1280]{1,0:T(8,128)(2,1)} %collective-permute-done.7, bf16[2560,5120]{0,1:T(8,128)(2,1)} %all-gather.2.cloned.1.call-done, bf16[768,2560]{0,1:T(8,128)(2,1)} %bitcast.15, s32[]{:T(128)S(6)} %select_n.43), kind=kOutput, calls=%fused_computation.36 | convolution fusion | flops 2519040000 | bytes 10485764 | tf_op jit(solution)/shard_map/dot_general | solution.py:170
  488.6 2.2 maximum_bitcast_fusion
  (19 shorter events, 0.1 us)
Async XLA Ops:
  6.5 188.2 %copy-start = (s32[32,4]{0,1:T(4,128)S(1)}, s32[32,4]{0,1:T(4,128)}, u32[]{:S(2)}) copy-start(s32[32,4]{0,1:T(4,128)} %param.16) | copy-start | bytes 1540
  6.5 382.6 %all-gather.2.cloned.1.call-start = ((), (), s32[]{:S(2)}) async-start(), calls=%async_computation.4 | async-start | bytes 27852800 | tf_op jit(solution)/shard_map/all_gather | solution.py:140
  7.3 8.9 %copy-start.3 = (f32[5120]{0:T(1024)S(1)}, f32[5120]{0:T(1024)}, u32[]{:S(2)}) copy-start(f32[5120]{0:T(1024)} %param.13) | copy-start | bytes 61444
  27.6 49.9 %all-to-all-start.1 = ((bf16[8,384,640]{2,1,0:T(8,128)(2,1)}), bf16[8,384,640]{2,1,0:T(8,128)(2,1)}, u32[]{:S(2)}, u32[]{:S(2)}) async-start(bf16[8,384,640]{2,1,0:T(8,128)(2,1)} %bitcast.23), calls=%async_computation.1 | async-start | bytes 7864320 | tf_op jit(solution)/shard_map/all_to_all | solution.py:130
  77.5 50.4 %all-to-all-start.2 = ((bf16[8,384,640]{2,1,0:T(8,128)(2,1)}), bf16[8,384,640]{2,1,0:T(8,128)(2,1)}, u32[]{:S(2)}, u32[]{:S(2)}) async-start(bf16[8,384,640]{2,1,0:T(8,128)(2,1)} %bitcast.22), calls=%async_computation.2 | async-start | bytes 7864320 | tf_op jit(solution)/shard_map/all_to_all | solution.py:130
  83.0 8.9 %copy-start.4 = (f32[5120]{0:T(1024)S(1)}, f32[5120]{0:T(1024)}, u32[]{:S(2)}) copy-start(f32[5120]{0:T(1024)} %param.12) | copy-start | bytes 61444
  128.0 68.3 %all-to-all-start = ((bf16[8,384,640]{2,1,0:T(8,128)(2,1)}), bf16[8,384,640]{2,1,0:T(8,128)(2,1)}, u32[]{:S(2)}, u32[]{:S(2)}) async-start(bf16[8,384,640]{2,1,0:T(8,128)(2,1)} %bitcast.21), calls=%async_computation | async-start | bytes 7864320 | tf_op jit(solution)/shard_map/all_to_all | solution.py:130
  137.5 57.4 %copy-start.2 = (s32[32]{0:T(128)S(1)}, s32[32]{0:T(128)}, u32[]{:S(2)}) copy-start(s32[32]{0:T(128)} %param.17) | copy-start | bytes 388
  137.5 87.8 %collective-permute-start = (bf16[1152,640]{1,0:T(8,128)(2,1)}, bf16[1152,640]{1,0:T(8,128)(2,1)S(1)}, u32[]{:S(2)}, u32[]{:S(2)}) collective-permute-start(bf16[1152,640]{1,0:T(8,128)(2,1)} %bitcast.5), channel_id=1, source_target_pairs={{0,4},{1,5},{2,6},{3,7},{4,8},{5,9},{6,10},{7,11},{8,12},{9,13},{1... | collective-permute-start | bytes 4423688 | tf_op jit(solution)/shard_map/ppermute | solution.py:22
  183.0 13.0 %copy-start.6 = (f32[20]{0:T(128)S(1)}, f32[20]{0:T(128)}, u32[]{:S(2)}) copy-start(f32[20]{0:T(128)} %param.14) | copy-start | bytes 244
  183.0 48.3 %collective-permute-start.1 = (bf16[1152,640]{1,0:T(8,128)(2,1)}, bf16[1152,640]{1,0:T(8,128)(2,1)S(1)}, u32[]{:S(2)}, u32[]{:S(2)}) collective-permute-start(bf16[1152,640]{1,0:T(8,128)(2,1)} %bitcast.7), channel_id=1, source_target_pairs={{4,0},{5,1},{6,2},{7,3},{8,4},{9,5},{10,6},{11,7},{12,8},{13,9},{1... | collective-permute-start | bytes 4423688 | tf_op jit(solution)/shard_map/ppermute | solution.py:22
  188.8 76.5 %collective-permute-start.2 = (bf16[1152,640]{1,0:T(8,128)(2,1)}, bf16[1152,640]{1,0:T(8,128)(2,1)}, u32[]{:S(2)}, u32[]{:S(2)}) collective-permute-start(bf16[1152,640]{1,0:T(8,128)(2,1)} %bitcast.10), channel_id=1, source_target_pairs={{0,4},{1,5},{2,6},{3,7},{4,8},{5,9},{6,10},{7,11},{8,12},{9,13},{1... | collective-permute-start | bytes 4423688 | tf_op jit(solution)/shard_map/ppermute | solution.py:22
  192.6 88.9 %collective-permute-start.3 = (bf16[1152,640]{1,0:T(8,128)(2,1)}, bf16[1152,640]{1,0:T(8,128)(2,1)}, u32[]{:S(2)}, u32[]{:S(2)}) collective-permute-start(bf16[1152,640]{1,0:T(8,128)(2,1)} %bitcast.12), channel_id=1, source_target_pairs={{4,0},{5,1},{6,2},{7,3},{8,4},{9,5},{10,6},{11,7},{12,8},{13,9},{1... | collective-permute-start | bytes 4423688 | tf_op jit(solution)/shard_map/ppermute | solution.py:22
  338.9 50.2 %all-to-all-start.3 = ((bf16[4,768,640]{1,2,0:T(8,128)(2,1)}), bf16[4,768,640]{1,2,0:T(8,128)(2,1)}, u32[]{:S(2)}, u32[]{:S(2)}) async-start(bf16[4,768,640]{1,2,0:T(8,128)(2,1)} %copy.18), calls=%async_computation.3 | async-start | bytes 7864320 | tf_op jit(solution)/shard_map/all_to_all | solution.py:156
  389.2 16.4 %copy-start.5 = (bf16[2560,5120]{0,1:T(8,128)(2,1)S(1)}, bf16[2560,5120]{0,1:T(8,128)(2,1)}, u32[]{:S(2)}) copy-start(bf16[2560,5120]{0,1:T(8,128)(2,1)} %all-gather.2.cloned.1.call-done) | copy-start | bytes 78643200
  395.5 24.7 %collective-permute-start.4 = (bf16[384,1280]{1,0:T(8,128)(2,1)S(1)}, bf16[384,1280]{1,0:T(8,128)(2,1)S(1)}, u32[]{:S(2)}, u32[]{:S(2)}) collective-permute-start(bf16[384,1280]{1,0:T(8,128)(2,1)S(1)} %fusion.24), channel_id=1, source_target_pairs={{0,16},{16,0},{1,17},{17,1},{2,18},{18,2},{3,19},{19,3},{4,20},{20... | collective-permute-start | bytes 2949128 | tf_op jit(solution)/shard_map/ppermute | solution.py:180
  403.9 37.5 %collective-permute-start.5 = (bf16[384,1280]{1,0:T(8,128)(2,1)}, bf16[384,1280]{1,0:T(8,128)(2,1)}, u32[]{:S(2)}, u32[]{:S(2)}) collective-permute-start(bf16[384,1280]{1,0:T(8,128)(2,1)} %fusion.33), channel_id=1, source_target_pairs={{0,16},{16,0},{1,17},{17,1},{2,18},{18,2},{3,19},{19,3},{4,20},{20... | collective-permute-start | bytes 2949128 | tf_op jit(solution)/shard_map/ppermute | solution.py:180
  410.8 51.7 %collective-permute-start.6 = (bf16[384,1280]{1,0:T(8,128)(2,1)}, bf16[384,1280]{1,0:T(8,128)(2,1)}, u32[]{:S(2)}, u32[]{:S(2)}) collective-permute-start(bf16[384,1280]{1,0:T(8,128)(2,1)} %fusion.42), channel_id=1, source_target_pairs={{0,16},{16,0},{1,17},{17,1},{2,18},{18,2},{3,19},{19,3},{4,20},{20... | collective-permute-start | bytes 2949128 | tf_op jit(solution)/shard_map/ppermute | solution.py:180
  416.4 65.8 %collective-permute-start.7 = (bf16[384,1280]{1,0:T(8,128)(2,1)}, bf16[384,1280]{1,0:T(8,128)(2,1)}, u32[]{:S(2)}, u32[]{:S(2)}) collective-permute-start(bf16[384,1280]{1,0:T(8,128)(2,1)} %fusion.51), channel_id=1, source_target_pairs={{0,16},{16,0},{1,17},{17,1},{2,18},{18,2},{3,19},{19,3},{4,20},{20... | collective-permute-start | bytes 2949128 | tf_op jit(solution)/shard_map/ppermute | solution.py:180
  482.2 8.6 %copy-start.1 = (s32[32,4]{0,1:T(4,128)S(1)}, s32[32,4]{0,1:T(4,128)}, u32[]{:S(2)}) copy-start(s32[32,4]{0,1:T(4,128)} %param.16) | copy-start | bytes 1540
Sparse Core Ops, SparseCore 0:
  9.0 264.0 all-gather.1
